TPU v7x, 128 devices: a whole 4x4x4 slice. The times are simulated.
128 devices in a mesh: ctx: 8 (over z, core), exp: 16 (over y, x).
Axes of the slice: x: 4, y: 4, z: 4, core: 2. Of those that a mesh axis runs over, the one named last changes fastest.
Arguments:
- mixer_input: bfloat16 [1024, 8192], P('ctx', 'exp'), may hold values from -6 to 6
- mixer_gate: bfloat16 [1024, 8192], P('ctx', 'exp'), may hold values from -6 to 6
- step_size: bfloat16 [1024, 8192], P('ctx', 'exp'), may hold values from 0.002 to 25
- write_coeffs: float32 [1024, 16], P('ctx'), may hold values from -1.5 to 1.5
- read_coeffs: float32 [1024, 16], P('ctx'), may hold values from -1.5 to 1.5
- decay_rates: float32 [8192, 16], P('exp'), may hold values from 0.01 to 0.6
- skip_scale: float32 [8192], P('exp'), may hold values from 0.5 to 1.5
- out_weight: bfloat16 [8192, 4096], P('exp', 'ctx'), may hold values from -0.0625 to 0.0625
- residual_in: bfloat16 [1024, 4096], P(('ctx', 'exp')), may hold values from -6 to 6
- norm_gain: float32 [4096], replicated, may hold values from 0.1 to 1.9
- expert_ids: int32 [1024, 2], P(('ctx', 'exp')), may hold values from 0 to 15, all different within a row; in each aligned block of 8 rows (0 to 7, 8 to 15, ...) at most 2 rows name the same one
- gate_weights: bfloat16 [1024, 2], P(('ctx', 'exp')), may hold values from 0.049804688 to 1
- up_weight: bfloat16 [16, 4096, 12288], P('exp', None, 'ctx'), may hold values from -0.09375 to 0.09375
- down_weight: bfloat16 [16, 12288, 4096], P('exp', 'ctx'), may hold values from -0.0546875 to 0.0546875
Outputs:
- layer_out: bfloat16 [1024, 4096], P(('ctx', 'exp'))
Inputs may be any that keep to these rules, and one draw needn't show every extreme that they name: `expert_ids`: each row names 2 different experts; among the 8 rows of one device no expert is named more than 2 times.
All inputs are finite; a program needn't handle non-finite values.
Results may differ from a plain program's by a relative error of at most 0.0057.
Values may be sent and summed in bfloat16 or wider, within the bound.
A program may use at most 128 MiB of HBM per device.

v0:
```python
import functools
import math

import jax
import jax.numpy as jnp
from jax import lax
from jax.experimental import pallas as pl
from jax.experimental.pallas import tpu as pltpu
from jax.sharding import PartitionSpec as P

MESH = pl.DeviceIdType.MESH
CAP = 2
EPSILON = 1e-05
LOG2E = math.log2(math.e)
F32 = jnp.float32
BF16 = jnp.bfloat16
STEPS = 16


def remote(src, dst, send_sem, recv_sem, device):
    return pltpu.make_async_remote_copy(
        src_ref=src,
        dst_ref=dst,
        send_sem=send_sem,
        recv_sem=recv_sem,
        device_id=device,
        device_id_type=MESH,
    )


def loop(count, body):
    def step(k, carry):
        body(k)
        return carry

    lax.fori_loop(0, count, step, 0)


def kernel(
    nctx,
    nexp,
    x_hbm,
    gate_hbm,
    step_hbm,
    write_hbm,
    read_hbm,
    rates_hbm,
    skip_hbm,
    ow_hbm,
    res_hbm,
    gain_hbm,
    ids_hbm,
    pairgate_hbm,
    up_hbm,
    down_hbm,
    out_ref,
    x_v,
    gate_v,
    step_v,
    write_v,
    read_v,
    rates_v,
    skip_v,
    res_v,
    gain_v,
    ids_v,
    pairgate_v,
    write_t,
    read_t,
    up_v,
    down_v,
    w_v,
    dt_f,
    u_f,
    wb_v,
    rb_v,
    rate2_v,
    h_v,
    hsend,
    hrecv,
    mixed_v,
    psend,
    precv,
    zsend,
    zrecv,
    stream_v,
    table_v,
    dsend,
    drecv,
    rows_v,
    acc_v,
    lifted_v,
    osend,
    orecv,
    okeep,
    rsend,
    rrecv,
    bsend,
    brecv,
    lsem,
    wsem,
    wswap,
    hs_sem,
    hr_sem,
    ms_sem,
    mr_sem,
    ps_sem,
    pr_sem,
    zs_sem,
    zr_sem,
    ds_sem,
    dr_sem,
    xs_sem,
    xr_sem,
    fs_sem,
    fr_sem,
    os_sem,
    or_sem,
    rs_sem,
    rr_sem,
    bs_sem,
    br_sem,
):
    i = lax.axis_index("ctx")
    j = lax.axis_index("exp")
    nz = nctx // 2
    z = lax.div(i, 2)
    c = lax.rem(i, 2)
    partner = (z * 2 + 1 - c, j)
    tokens, channels = x_hbm.shape
    states = write_hbm.shape[0]
    mine, width = res_hbm.shape
    block = width // nctx
    hidden = up_hbm.shape[1]
    chunks = nctx
    slots = nexp * CAP
    half = nz * slots

    def at_z(zz):
        return (zz * 2 + c, j)

    def at_e(e):
        return (i, e)

    def z_next(k):
        return lax.rem(z + k, nz)

    def e_next(k):
        return lax.rem(j + k, nexp)

    small = [
        (write_hbm, write_v),
        (read_hbm, read_v),
        (rates_hbm, rates_v),
        (step_hbm, step_v),
        (x_hbm, x_v),
        (gate_hbm, gate_v),
        (skip_hbm, skip_v),
        (res_hbm, res_v),
        (gain_hbm, gain_v),
        (ids_hbm, ids_v),
        (pairgate_hbm, pairgate_v),
        (ow_hbm, w_v.at[c]),
    ]
    small = [
        pltpu.make_async_copy(src, dst, lsem.at[n]) for n, (src, dst) in enumerate(small)
    ]
    for copy in small:
        copy.start()

    barrier = pltpu.get_barrier_semaphore()

    def greet_ctx(k):
        pl.semaphore_signal(
            barrier, inc=1, device_id=(lax.rem(i + k + 1, nctx), j), device_id_type=MESH
        )

    def greet_exp(k):
        pl.semaphore_signal(barrier, inc=1, device_id=at_e(e_next(k + 1)), device_id_type=MESH)

    loop(nctx - 1, greet_ctx)
    loop(nexp - 1, greet_exp)

    def up_copy(k):
        part = pl.ds(pl.multiple_of(k * block, block), block)
        return pltpu.make_async_copy(up_hbm.at[part], up_v.at[part], wsem.at[0, k])

    depth = hidden // chunks

    def down_copy(k):
        part = pl.ds(pl.multiple_of(k * depth, depth), depth)
        return pltpu.make_async_copy(down_hbm.at[part], down_v.at[part], wsem.at[1, k])

    loop(chunks, lambda k: up_copy(k).start())
    loop(chunks, lambda k: down_copy(k).start())

    small[0].wait()
    small[1].wait()
    write_t[...] = write_v[...].T
    read_t[...] = read_v[...].T
    diagonal = lax.broadcasted_iota(jnp.int32, (1, states, states), 1) == lax.broadcasted_iota(
        jnp.int32, (1, states, states), 2
    )

    def spread(n):
        part = pl.ds(pl.multiple_of(n * STEPS, STEPS), STEPS)
        for source, wide in ((write_t, wb_v), (read_t, rb_v)):
            rows = jnp.broadcast_to(source[part, :][:, None, :], (STEPS, states, states))
            picked = jnp.sum(jnp.where(diagonal, rows, 0.0), axis=2, keepdims=True)
            wide[part] = jnp.broadcast_to(picked, (STEPS, states, 128))

    loop(tokens // STEPS, spread)
    small[2].wait()
    rate2_v[...] = rates_v[...] * (-LOG2E)
    small[3].wait()
    small[4].wait()

    def widen(n):
        part = pl.ds(pl.multiple_of(n * STEPS, STEPS), STEPS)
        steps = step_v[part, :].astype(F32)
        dt_f[part, :] = steps
        u_f[part, :] = steps * x_v[part, :].astype(F32)

    loop(tokens // STEPS, widen)
    copies = channels // 128

    def advance(h, t, rate2):
        decay = jnp.exp2(dt_f[pl.ds(t, 1), :] * rate2)
        push = u_f[pl.ds(t, 1), :] * jnp.concatenate([wb_v[t]] * copies, axis=1)
        return decay * h + push

    def first(n, carry):
        h, total = carry
        rate2 = rate2_v[...]
        for r in range(STEPS):
            h = advance(h, n * STEPS + r, rate2)
        part = pl.ds(pl.multiple_of(n * STEPS, STEPS), STEPS)
        return h, total + jnp.sum(dt_f[part, :], axis=0, keepdims=True)

    h, total = lax.fori_loop(
        0,
        tokens // STEPS,
        first,
        (jnp.zeros((states, channels), F32), jnp.zeros((1, channels), F32)),
    )
    hsend[0:states, :] = h
    hsend[states : states + 8, :] = jnp.broadcast_to(total, (8, channels))

    pl.semaphore_wait(barrier, nctx + nexp - 2)

    def state_copy(k):
        return remote(
            hsend, hrecv.at[i], hs_sem.at[k], hr_sem.at[i], (lax.rem(i + k, nctx), j)
        )

    for k in range(1, nctx):

        @pl.when(i + k < nctx)
        def _():
            state_copy(k).start()

    small[11].wait()
    swap = remote(w_v.at[c], w_v.at[c], wswap.at[0], wswap.at[1], partner)
    swap.start()

    h_v[...] = jnp.zeros_like(h_v)
    for k in range(nctx - 1):

        @pl.when(k < i)
        def _():
            remote(hsend, hrecv.at[k], hs_sem.at[0], hr_sem.at[k], partner).wait_recv()
            gone = jnp.exp2(rate2_v[...] * hrecv[k, states : states + 1, :])
            h_v[...] = gone * h_v[...] + hrecv[k, 0:states, :]

    small[5].wait()
    small[6].wait()

    def second(n, h):
        part = pl.ds(pl.multiple_of(n * STEPS, STEPS), STEPS)
        rate2 = rate2_v[...]
        reads = []
        for r in range(STEPS):
            t = n * STEPS + r
            h = advance(h, t, rate2)
            seen = h * jnp.concatenate([rb_v[t]] * copies, axis=1)
            reads.append(jnp.sum(seen, axis=0, keepdims=True))
        readout = jnp.concatenate(reads, axis=0)
        readout = readout + skip_v[...] * x_v[part, :].astype(F32)
        gate = gate_v[part, :].astype(F32)
        mixed_v[z, part, :] = (readout * (gate / (1.0 + jnp.exp(-gate)))).astype(BF16)
        return h

    lax.fori_loop(0, tokens // STEPS, second, h_v[...])

    def mixed_copy(k):
        return remote(
            mixed_v.at[z], mixed_v.at[z], ms_sem.at[k], mr_sem.at[z], at_z(z_next(k))
        )

    for k in range(1, nz):
        mixed_copy(k).start()

    pair_rows = 2 * mine

    def psum_copy(zz, k):
        part = pl.ds(pl.multiple_of(zz * pair_rows, pair_rows), pair_rows)
        e = e_next(k)
        return remote(
            psend.at[e, part],
            precv.at[j, part],
            ps_sem.at[zz, k],
            pr_sem.at[zz, j],
            at_e(e),
        )

    swap.wait_recv()

    def project(k):
        zz = z_next(k)

        @pl.when(k > 0)
        def _():
            remote(
                mixed_v.at[zz], mixed_v.at[zz], ms_sem.at[0], mr_sem.at[zz], partner
            ).wait_recv()

        part = pl.ds(pl.multiple_of(zz * pair_rows, pair_rows), pair_rows)
        sides = [
            jnp.dot(mixed_v[zz], w_v[side], preferred_element_type=F32).reshape(nexp, mine, block)
            for side in range(2)
        ]
        psend[:, part, :] = jnp.concatenate(sides, axis=1).astype(BF16)
        loop(nexp - 1, lambda e: psum_copy(zz, e + 1).start())

    loop(nz, project)

    total_rows = nz * pair_rows

    def gather_sum(k, total):
        e = e_next(k)

        def arrive(zz):
            part = pl.ds(pl.multiple_of(zz * pair_rows, pair_rows), pair_rows)
            remote(
                psend.at[e, part], precv.at[e, part], ps_sem.at[zz, 0], pr_sem.at[zz, e], partner
            ).wait_recv()

        loop(nz, arrive)
        return total + precv[e].astype(F32)

    sums = lax.fori_loop(1, nexp, gather_sum, psend[j].astype(F32))
    zsend[...] = sums.reshape(nz, pair_rows, block)
    zrecv[z] = zsend[z]

    def zsum_copy(k):
        zz = z_next(k)
        return remote(zsend.at[zz], zrecv.at[z], zs_sem.at[k], zr_sem.at[z], at_z(zz))

    for k in range(1, nz):
        zsum_copy(k).start()

    for n in (7, 8, 9, 10):
        small[n].wait()
    lanes = lax.broadcasted_iota(jnp.int32, (mine, 128), 1)
    square = lax.broadcasted_iota(jnp.int32, (mine, mine), 0) == lax.broadcasted_iota(
        jnp.int32, (mine, mine), 1
    )

    def column_of(row):
        return jnp.sum(jnp.where(square, row.astype(F32), 0.0), axis=1, keepdims=True)

    first_id = column_of(ids_v[0:1, :]).astype(jnp.int32)
    second_id = column_of(ids_v[1:2, :]).astype(jnp.int32)
    first_hot = (lanes == first_id).astype(F32)
    second_hot = (lanes == second_id).astype(F32)
    earlier = (
        lax.broadcasted_iota(jnp.int32, (mine, mine), 0)
        > lax.broadcasted_iota(jnp.int32, (mine, mine), 1)
    ).astype(F32)
    before = jnp.dot(earlier, first_hot + second_hot, preferred_element_type=F32)
    stacked = chunks * mine
    places = nexp * chunks * CAP
    column = lax.broadcasted_iota(jnp.int32, (stacked, places), 1)
    row = lax.broadcasted_iota(jnp.int32, (stacked, places), 0)
    column_slot = lax.div(column, chunks * CAP) * CAP + lax.rem(column, CAP)
    same_block = lax.rem(lax.div(column, CAP), chunks) == lax.div(row, mine)
    table = jnp.zeros((stacked, places), F32)
    gated = jnp.zeros((stacked, places), F32)
    pair_gates = pairgate_v[...].astype(F32)
    for choice, (ident, hot) in enumerate(((first_id, first_hot), (second_id, second_hot))):
        rank = jnp.sum(before * hot, axis=1, keepdims=True).astype(jnp.int32)
        slot = jnp.concatenate([ident * CAP + rank] * chunks, axis=0)
        taken = jnp.where(same_block & (column_slot == slot), 1.0, 0.0)
        weight = jnp.concatenate([column_of(pair_gates[choice : choice + 1, :])] * chunks, axis=0)
        table = table + taken
        gated = gated + taken * weight
    table_v[...] = gated.astype(BF16)
    table_down = table.T.astype(BF16)

    for k in range(1, nz):
        zz = z_next(k)
        remote(zsend.at[zz], zrecv.at[zz], zs_sem.at[0], zr_sem.at[zz], partner).wait_recv()

    def stack(wide):
        return jnp.concatenate(
            [wide[:, k * block : (k + 1) * block] for k in range(chunks)], axis=0
        )

    res = stack(res_v[...].astype(F32))
    gain = stack(jnp.broadcast_to(gain_v[...], (mine, width)))
    stream = (res + zrecv[...].reshape(stacked, block)).astype(BF16).astype(F32)
    stream_v[...] = stream
    squares = jnp.sum(stream * stream, axis=1, keepdims=True).reshape(chunks, mine, 1)
    scale = lax.rsqrt(jnp.sum(squares, axis=0) / width + EPSILON)
    normed = (stream * jnp.concatenate([scale] * chunks, axis=0) * gain).astype(BF16)

    pack = chunks * CAP
    dsend[...] = (
        jnp.dot(table_down, normed, preferred_element_type=F32)
        .astype(BF16)
        .reshape(nexp, pack, block)
    )

    def dispatch_copy(k):
        e = e_next(k)
        return remote(dsend.at[e], drecv.at[j], ds_sem.at[k], dr_sem.at[j], at_e(e))

    loop(nexp - 1, lambda k: dispatch_copy(k + 1).start())
    drecv[j] = dsend[j]
    source = lax.broadcasted_iota(jnp.int32, (places, places), 1)
    target = lax.broadcasted_iota(jnp.int32, (places, places), 0)
    place = lax.rem(source, CAP)
    chunk_of = lax.rem(lax.div(source, CAP), chunks)
    from_device = lax.div(source, pack)
    order = (chunk_of * slots + from_device * CAP + place == target).astype(F32).astype(BF16)

    def dispatch_arrive(k):
        e = e_next(k + 1)
        remote(dsend.at[e], drecv.at[e], ds_sem.at[0], dr_sem.at[e], partner).wait_recv()

    loop(nexp - 1, dispatch_arrive)
    arranged = jnp.dot(order, drecv[...].reshape(places, block), preferred_element_type=F32)
    own = pl.ds(pl.multiple_of(z * slots, slots), slots)
    rows_v[:, own, :] = arranged.astype(BF16).reshape(chunks, slots, block)

    def rows_part(zz):
        return pl.ds(pl.multiple_of(zz * slots, slots), slots)

    def far_part(zz):
        return pl.ds(pl.multiple_of(half + zz * slots, slots), slots)

    def rows_copy(k, n):
        return remote(
            rows_v.at[k, own],
            rows_v.at[k, own],
            xs_sem.at[k, n],
            xr_sem.at[k, z],
            at_z(z_next(n)),
        )

    def forward_copy(k, zz):
        return remote(
            rows_v.at[k, rows_part(zz)],
            rows_v.at[k, far_part(zz)],
            fs_sem.at[k, zz],
            fr_sem.at[k, zz],
            partner,
        )

    def rows_out(k):
        for n in range(1, nz):
            rows_copy(k, n).start()
        forward_copy(k, z).start()

    loop(chunks, rows_out)

    def rows_arrive(k):
        for n in range(1, nz):
            zz = z_next(n)
            part = rows_part(zz)
            remote(
                rows_v.at[k, part], rows_v.at[k, part], xs_sem.at[k, 0], xr_sem.at[k, zz], partner
            ).wait_recv()
            forward_copy(k, zz).start()

    tile = 512 if hidden % 512 == 0 else hidden
    tiles = hidden // tile

    def lift(k):
        for zz in range(nz):
            forward_copy(k, zz).wait_recv()
        up_copy(k).wait()
        part = pl.ds(pl.multiple_of(k * block, block), block)

        def one(n):
            columns = pl.ds(pl.multiple_of(n * tile, tile), tile)
            product = jnp.dot(rows_v[k], up_v[part, columns], preferred_element_type=F32)

            @pl.when(k == 0)
            def _():
                acc_v[:, columns] = product

            @pl.when(k > 0)
            def _():
                acc_v[:, columns] += product

        loop(tiles, one)

    rows_arrive(0)

    def up_step(k):
        rows_arrive(k + 1)
        lift(k)

    loop(chunks - 1, up_step)
    lift(chunks - 1)

    def activate(n):
        columns = pl.ds(pl.multiple_of(n * tile, tile), tile)
        lifted = acc_v[:, columns]
        lifted_v[:, columns] = (lifted / (1.0 + jnp.exp(-lifted))).astype(BF16)

    loop(tiles, activate)
    loop(chunks, lambda k: down_copy(k).wait())

    def pair_copy(k):
        return remote(osend.at[k], orecv.at[k], os_sem.at[k], or_sem.at[k], partner)

    def back_copy(k, n):
        zz = z_next(n)
        return remote(
            rsend.at[k, zz], rrecv.at[k, z], rs_sem.at[k, n], rr_sem.at[k, z], at_z(zz)
        )

    def lower(k):
        columns = pl.ds(pl.multiple_of(k * block, block), block)
        product = jnp.dot(lifted_v[...], down_v[:, columns], preferred_element_type=F32)
        okeep[k] = product[0:half]
        osend[k] = product[half : 2 * half].astype(BF16)
        pair_copy(k).start()

    def send_back(k):
        pair_copy(k).wait_recv()
        both = okeep[k] + orecv[k].astype(F32)
        rsend[k] = both.astype(BF16).reshape(nz, slots, block)
        for n in range(1, nz):
            back_copy(k, n).start()
        rrecv[k, z] = rsend[k, z]

    lower(0)

    def down_step(k):
        lower(k + 1)
        send_back(k)

    loop(chunks - 1, down_step)
    send_back(chunks - 1)

    def back_arrive(k):
        for n in range(1, nz):
            zz = z_next(n)
            remote(
                rsend.at[k, zz], rrecv.at[k, zz], rs_sem.at[k, 0], rr_sem.at[k, zz], partner
            ).wait_recv()
        total = rrecv[k, 0].astype(F32)
        for zz in range(1, nz):
            total = total + rrecv[k, zz].astype(F32)
        rrecv[k, 0] = total.astype(BF16)

    loop(chunks, back_arrive)
    summed = rrecv[:, 0].reshape(places, block)
    unorder = (
        lax.rem(lax.div(target, CAP), chunks) * slots
        + lax.div(target, pack) * CAP
        + lax.rem(target, CAP)
        == source
    ).astype(F32).astype(BF16)
    bsend[...] = (
        jnp.dot(unorder, summed, preferred_element_type=F32)
        .astype(BF16)
        .reshape(nexp, pack, block)
    )

    def return_copy(k):
        e = e_next(k)
        return remote(bsend.at[e], brecv.at[j], bs_sem.at[k], br_sem.at[j], at_e(e))

    loop(nexp - 1, lambda k: return_copy(k + 1).start())
    brecv[j] = bsend[j]

    def return_arrive(k):
        e = e_next(k + 1)
        remote(bsend.at[e], brecv.at[e], bs_sem.at[0], br_sem.at[e], partner).wait_recv()

    loop(nexp - 1, return_arrive)
    combined = jnp.dot(
        table_v[...], brecv[...].reshape(places, block), preferred_element_type=F32
    )
    result = (stream_v[...] + combined).astype(BF16)
    for k in range(chunks):
        out_ref[:, k * block : (k + 1) * block] = result[k * mine : (k + 1) * mine]

    for k in range(1, nctx):

        @pl.when(i + k < nctx)
        def _():
            state_copy(k).wait_send()

    swap.wait_send()
    for k in range(1, nz):
        mixed_copy(k).wait_send()
        zsum_copy(k).wait_send()

    def drain_exp(k):
        dispatch_copy(k + 1).wait_send()
        return_copy(k + 1).wait_send()
        loop(nz, lambda zz: psum_copy(zz, k + 1).wait_send())

    loop(nexp - 1, drain_exp)

    def drain_chunk(k):
        pair_copy(k).wait_send()
        for n in range(1, nz):
            rows_copy(k, n).wait_send()
            back_copy(k, n).wait_send()
        for zz in range(nz):
            forward_copy(k, zz).wait_send()

    loop(chunks, drain_chunk)


def shards(nctx, nexp, *arrays):
    (
        mixer_input,
        mixer_gate,
        step_size,
        write_coeffs,
        read_coeffs,
        decay_rates,
        skip_scale,
        out_weight,
        residual_in,
        norm_gain,
        expert_ids,
        gate_weights,
        up_weight,
        down_weight,
    ) = arrays
    tokens, channels = mixer_input.shape
    states = write_coeffs.shape[1]
    mine, width = residual_in.shape
    hidden = up_weight.shape[2]
    nz = nctx // 2
    block = width // nctx
    chunks = nctx
    slots = nexp * CAP
    pack = chunks * CAP
    operands = (
        mixer_input,
        mixer_gate,
        step_size,
        write_coeffs.T,
        read_coeffs.T,
        decay_rates.T,
        skip_scale.reshape(1, channels),
        out_weight,
        residual_in,
        norm_gain.reshape(1, width),
        expert_ids.T,
        gate_weights.T,
        up_weight.reshape(width, hidden),
        down_weight.reshape(hidden, width),
    )
    dma = pltpu.SemaphoreType.DMA
    scratch = [
        pltpu.VMEM((tokens, channels), BF16),
        pltpu.VMEM((tokens, channels), BF16),
        pltpu.VMEM((tokens, channels), BF16),
        pltpu.VMEM((states, tokens), F32),
        pltpu.VMEM((states, tokens), F32),
        pltpu.VMEM((states, channels), F32),
        pltpu.VMEM((1, channels), F32),
        pltpu.VMEM((mine, width), BF16),
        pltpu.VMEM((1, width), F32),
        pltpu.VMEM((2, mine), jnp.int32),
        pltpu.VMEM((2, mine), BF16),
        pltpu.VMEM((tokens, states), F32),
        pltpu.VMEM((tokens, states), F32),
        pltpu.VMEM((width, hidden), BF16),
        pltpu.VMEM((hidden, width), BF16),
        pltpu.VMEM((2, channels, block), BF16),
        pltpu.VMEM((tokens, channels), F32),
        pltpu.VMEM((tokens, channels), F32),
        pltpu.VMEM((tokens, states, 128), F32),
        pltpu.VMEM((tokens, states, 128), F32),
        pltpu.VMEM((states, channels), F32),
        pltpu.VMEM((states, channels), F32),
        pltpu.VMEM((states + 8, channels), F32),
        pltpu.VMEM((nctx, states + 8, channels), F32),
        pltpu.VMEM((nz, tokens, channels), BF16),
        pltpu.VMEM((nexp, nz * 2 * mine, block), BF16),
        pltpu.VMEM((nexp, nz * 2 * mine, block), BF16),
        pltpu.VMEM((nz, 2 * mine, block), F32),
        pltpu.VMEM((nz, 2 * mine, block), F32),
        pltpu.VMEM((chunks * mine, block), F32),
        pltpu.VMEM((chunks * mine, nexp * pack), BF16),
        pltpu.VMEM((nexp, pack, block), BF16),
        pltpu.VMEM((nexp, pack, block), BF16),
        pltpu.VMEM((chunks, nctx * slots, block), BF16),
        pltpu.VMEM((nctx * slots, hidden), F32),
        pltpu.VMEM((nctx * slots, hidden), BF16),
        pltpu.VMEM((chunks, nz * slots, block), BF16),
        pltpu.VMEM((chunks, nz * slots, block), BF16),
        pltpu.VMEM((chunks, nz * slots, block), F32),
        pltpu.VMEM((chunks, nz, slots, block), BF16),
        pltpu.VMEM((chunks, nz, slots, block), BF16),
        pltpu.VMEM((nexp, pack, block), BF16),
        pltpu.VMEM((nexp, pack, block), BF16),
        dma((12,)),
        dma((2, chunks)),
        dma((2,)),
        dma((nctx,)),
        dma((nctx,)),
        dma((nz,)),
        dma((nz,)),
        dma((nz, nexp)),
        dma((nz, nexp)),
        dma((nz,)),
        dma((nz,)),
        dma((nexp,)),
        dma((nexp,)),
        dma((chunks, nz)),
        dma((chunks, nz)),
        dma((chunks, nz)),
        dma((chunks, nz)),
        dma((chunks,)),
        dma((chunks,)),
        dma((chunks, nz)),
        dma((chunks, nz)),
        dma((nexp,)),
        dma((nexp,)),
    ]
    return pl.pallas_call(
        functools.partial(kernel, nctx, nexp),
        out_shape=jax.ShapeDtypeStruct((mine, width), BF16),
        in_specs=[pl.BlockSpec(memory_space=pl.ANY)] * len(operands),
        out_specs=pl.BlockSpec(memory_space=pltpu.VMEM),
        scratch_shapes=scratch,
        compiler_params=pltpu.CompilerParams(
            collective_id=0, has_side_effects=True, vmem_limit_bytes=60 * 2**20
        ),
    )(*operands)


def solution(mesh):
    return jax.shard_map(
        functools.partial(shards, mesh.shape["ctx"], mesh.shape["exp"]),
        mesh=mesh,
        in_specs=(
            P("ctx", "exp"),
            P("ctx", "exp"),
            P("ctx", "exp"),
            P("ctx", None),
            P("ctx", None),
            P("exp", None),
            P("exp"),
            P("exp", "ctx"),
            P(("ctx", "exp"), None),
            P(),
            P(("ctx", "exp"), None),
            P(("ctx", "exp"), None),
            P("exp", None, "ctx"),
            P("exp", "ctx", None),
        ),
        out_specs=P(("ctx", "exp"), None),
        check_vma=False,
    )
```

profile of v0, /device:TPU:0, one launch (start us, length us, event | category | flops | bytes accessed | tf_op | source)
XLA Modules:
  0.0 90.0 jit_solution(17392014215826228590)
XLA Ops:
  0.0 88.6 %shard_map.136 = bf16[8,4096]{1,0:T(8,128)(2,1)} custom-call(bf16[128,512]{1,0:T(8,128)(2,1)} %x_hbm.1, bf16[128,512]{1,0:T(8,128)(2,1)} %gate_hbm.1, bf16[128,512]{1,0:T(8,128)(2,1)} %step_hbm.1, f32[16,128]{1,0:T(8,128)} %bitcast.13, f32[16,128]{1,0:T(8,128)} %bitcast.14, f32[16,512]{1,0:T(8,128)} %bitcast.11, f32[1,512]{1,0:T(1,128)} %bitcast.15, ...), custom_call_target="tpu_custom_call" | custom-call | tf_op jit(solution)/shard_map/pallas_call | solution.py:743
  88.6 1.5 %copy.16 = bf16[8,4096]{1,0:T(8,128)(2,1)} copy(bf16[8,4096]{1,0:T(8,128)(2,1)} %shard_map.136) | data formatting | bytes 131072
where the time goes:
time: 90.2 us; the launch traced here: 90 us
  Pallas kernels  88.6 us (98%)
  local copies, waits for them, and re-layouts  1.47 us (2%)
    pallas_call x1, Pallas kernels, shards(): pl.pallas_call(functools.partial(kernel, nctx, nexp), out_shape=jax.Shape...  88.6 us

commit v1 on v0

v1 whole, which is shorter than its diff:
```python
import functools
import math

import jax
import jax.numpy as jnp
from jax import lax
from jax.experimental import pallas as pl
from jax.experimental.pallas import tpu as pltpu
from jax.sharding import PartitionSpec as P

MESH = pl.DeviceIdType.MESH
CAP = 2
EPSILON = 1e-05
LOG2E = math.log2(math.e)
F32 = jnp.float32
BF16 = jnp.bfloat16
STEPS = 16


def remote(src, dst, send_sem, recv_sem, device):
    return pltpu.make_async_remote_copy(
        src_ref=src,
        dst_ref=dst,
        send_sem=send_sem,
        recv_sem=recv_sem,
        device_id=device,
        device_id_type=MESH,
    )


def loop(count, body):
    def step(k, carry):
        body(k)
        return carry

    lax.fori_loop(0, count, step, 0)


def kernel(
    nctx,
    nexp,
    x_hbm,
    gate_hbm,
    step_hbm,
    write_hbm,
    read_hbm,
    rates_hbm,
    skip_hbm,
    ow_hbm,
    res_hbm,
    gain_hbm,
    ids_hbm,
    pairgate_hbm,
    up_hbm,
    down_hbm,
    out_ref,
    x_v,
    gate_v,
    step_v,
    write_v,
    read_v,
    rates_v,
    skip_v,
    res_v,
    gain_v,
    ids_v,
    pairgate_v,
    write_t,
    read_t,
    up_v,
    down_v,
    w_v,
    dt_f,
    u_f,
    wb_v,
    rb_v,
    rate2_v,
    h_v,
    hsend,
    hrecv,
    tsend,
    trecv,
    meta_v,
    metas,
    mixed_v,
    near_send,
    near_recv,
    far_send,
    far_recv,
    stream_v,
    table_v,
    gated_v,
    order_v,
    nrows,
    lsend,
    lrecv,
    qsend,
    qrecv,
    rows_v,
    acc_v,
    lifted_v,
    osend,
    orecv,
    okeep,
    rsum,
    lsum,
    rsend,
    rrecv,
    qsend2,
    qrecv2,
    lsend2,
    lrecv2,
    csend,
    crecv,
    lsem,
    wsem,
    wswap,
    hs_sem,
    hr_sem,
    ms_sem,
    mr_sem,
    ps_sem,
    pr_sem,
    zs_sem,
    zr_sem,
    mt_sem,
    ns_sem,
    nr_sem,
    ls_sem,
    lr_sem,
    qs_sem,
    qr_sem,
    xs_sem,
    xr_sem,
    fs_sem,
    fr_sem,
    gs_sem,
    gr_sem,
    os_sem,
    or_sem,
    rs_sem,
    rr_sem,
    hq_sem,
    hl_sem,
    cs_sem,
):
    i = lax.axis_index("ctx")
    j = lax.axis_index("exp")
    nz = nctx // 2
    z = lax.div(i, 2)
    c = lax.rem(i, 2)
    nx = math.isqrt(nexp)
    y, x = lax.div(j, nx), lax.rem(j, nx)
    partner = (z * 2 + 1 - c, j)
    tokens, channels = x_hbm.shape
    states = write_hbm.shape[0]
    mine, width = res_hbm.shape
    block = width // nctx
    hidden = up_hbm.shape[1]
    chunks = nctx
    parts = 2 * chunks
    slots = nexp * CAP
    half = nz * slots

    def at_z(zz):
        return (zz * 2 + c, j)

    def at_e(e):
        return (i, e)

    def z_next(k):
        return lax.rem(z + k, nz)

    def e_next(k):
        return lax.rem(j + k, nexp)

    small = [
        (write_hbm, write_v),
        (read_hbm, read_v),
        (rates_hbm, rates_v),
        (step_hbm, step_v),
        (x_hbm, x_v),
        (gate_hbm, gate_v),
        (skip_hbm, skip_v),
        (res_hbm, res_v),
        (gain_hbm, gain_v),
        (ids_hbm, ids_v),
        (pairgate_hbm, pairgate_v),
        (ow_hbm, w_v.at[c]),
    ]
    small = [
        pltpu.make_async_copy(src, dst, lsem.at[n]) for n, (src, dst) in enumerate(small)
    ]
    for copy in small:
        copy.start()

    barrier = pltpu.get_barrier_semaphore()

    def greet_ctx(k):
        pl.semaphore_signal(
            barrier, inc=1, device_id=(lax.rem(i + k + 1, nctx), j), device_id_type=MESH
        )

    loop(nctx - 1, greet_ctx)
    for k in range(1, nx):
        for e in (y * nx + lax.rem(x + k, nx), lax.rem(y + k, nx) * nx + x):
            pl.semaphore_signal(barrier, inc=1, device_id=at_e(e), device_id_type=MESH)

    def up_copy(k):
        part = pl.ds(pl.multiple_of(k * block, block), block)
        return pltpu.make_async_copy(up_hbm.at[part], up_v.at[part], wsem.at[0, k])

    depth = hidden // chunks

    def down_copy(k):
        part = pl.ds(pl.multiple_of(k * depth, depth), depth)
        return pltpu.make_async_copy(down_hbm.at[part], down_v.at[part], wsem.at[1, k])

    loop(chunks, lambda k: up_copy(k).start())
    loop(chunks, lambda k: down_copy(k).start())

    small[0].wait()
    small[1].wait()
    write_t[...] = write_v[...].T
    read_t[...] = read_v[...].T
    diagonal = lax.broadcasted_iota(jnp.int32, (1, states, states), 1) == lax.broadcasted_iota(
        jnp.int32, (1, states, states), 2
    )

    def spread(n):
        part = pl.ds(pl.multiple_of(n * STEPS, STEPS), STEPS)
        for source, wide in ((write_t, wb_v), (read_t, rb_v)):
            rows = jnp.broadcast_to(source[part, :][:, None, :], (STEPS, states, states))
            picked = jnp.sum(jnp.where(diagonal, rows, 0.0), axis=2, keepdims=True)
            wide[part] = jnp.broadcast_to(picked, (STEPS, states, 128))

    loop(tokens // STEPS, spread)
    small[2].wait()
    rate2_v[...] = rates_v[...] * (-LOG2E)
    small[3].wait()
    small[4].wait()

    def widen(n):
        part = pl.ds(pl.multiple_of(n * STEPS, STEPS), STEPS)
        steps = step_v[part, :].astype(F32)
        dt_f[part, :] = steps
        u_f[part, :] = steps * x_v[part, :].astype(F32)

    loop(tokens // STEPS, widen)
    copies = channels // 128

    def advance(h, t, rate2):
        decay = jnp.exp2(dt_f[pl.ds(t, 1), :] * rate2)
        push = u_f[pl.ds(t, 1), :] * jnp.concatenate([wb_v[t]] * copies, axis=1)
        return decay * h + push

    def first(n, carry):
        h, total = carry
        rate2 = rate2_v[...]
        for r in range(STEPS):
            h = advance(h, n * STEPS + r, rate2)
        part = pl.ds(pl.multiple_of(n * STEPS, STEPS), STEPS)
        return h, total + jnp.sum(dt_f[part, :], axis=0, keepdims=True)

    h, total = lax.fori_loop(
        0,
        tokens // STEPS,
        first,
        (jnp.zeros((states, channels), F32), jnp.zeros((1, channels), F32)),
    )
    hsend[...] = h.astype(BF16)
    folded = jnp.concatenate([total[:, q * 128 : (q + 1) * 128] for q in range(copies)], axis=0)
    tsend[...] = jnp.concatenate([folded] * (8 // copies), axis=0)
    meta_v[...] = jnp.zeros_like(meta_v)
    small[9].wait()
    small[10].wait()
    meta_v[0:2, 0:mine] = ids_v[...].astype(F32)
    meta_v[2:4, 0:mine] = pairgate_v[...].astype(F32)

    pl.semaphore_wait(barrier, nctx - 1 + 2 * (nx - 1))

    def state_copies(k):
        device = (lax.rem(i + k, nctx), j)
        return (
            remote(tsend, trecv.at[i], hs_sem.at[0, k], hr_sem.at[0, i], device),
            remote(hsend, hrecv.at[i], hs_sem.at[1, k], hr_sem.at[1, i], device),
        )

    for k in range(1, nctx):

        @pl.when(i + k < nctx)
        def _():
            for copy in state_copies(k):
                copy.start()

    def drain_states():
        for k in range(1, nctx):

            @pl.when(i + k < nctx)
            def _():
                for copy in state_copies(k):
                    copy.wait_send()

    sent = [drain_states]

    def meta_copy(k):
        return remote(
            meta_v, metas.at[z], mt_sem.at[0, k], mt_sem.at[1, z], at_z(z_next(k))
        )

    small[11].wait()
    swap = remote(w_v.at[c], w_v.at[c], wswap.at[0], wswap.at[1], partner)
    swap.start()
    sent.append(swap.wait_send)

    h_v[...] = jnp.zeros_like(h_v)
    for k in range(nctx - 1):

        @pl.when(k < i)
        def _():
            remote(tsend, trecv.at[k], hs_sem.at[0, 0], hr_sem.at[0, k], partner).wait_recv()
            remote(hsend, hrecv.at[k], hs_sem.at[1, 0], hr_sem.at[1, k], partner).wait_recv()
            passed = jnp.concatenate([trecv[k, q : q + 1, :] for q in range(copies)], axis=1)
            h_v[...] = jnp.exp2(rate2_v[...] * passed) * h_v[...] + hrecv[k].astype(F32)

    for k in range(1, nz):
        meta_copy(k).start()
    metas[z] = meta_v[...]
    sent.append(lambda: [meta_copy(k).wait_send() for k in range(1, nz)])

    small[5].wait()
    small[6].wait()

    def second(n, h):
        part = pl.ds(pl.multiple_of(n * STEPS, STEPS), STEPS)
        rate2 = rate2_v[...]
        reads = []
        for r in range(STEPS):
            t = n * STEPS + r
            h = advance(h, t, rate2)
            seen = h * jnp.concatenate([rb_v[t]] * copies, axis=1)
            reads.append(jnp.sum(seen, axis=0, keepdims=True))
        readout = jnp.concatenate(reads, axis=0)
        readout = readout + skip_v[...] * x_v[part, :].astype(F32)
        gate = gate_v[part, :].astype(F32)
        mixed_v[z, part, :] = (readout * (gate / (1.0 + jnp.exp(-gate)))).astype(BF16)
        return h

    lax.fori_loop(0, tokens // STEPS, second, h_v[...])

    def mixed_copy(k):
        return remote(
            mixed_v.at[z], mixed_v.at[z], ms_sem.at[k], mr_sem.at[z], at_z(z_next(k))
        )

    for k in range(1, nz):
        mixed_copy(k).start()
    sent.append(lambda: [mixed_copy(k).wait_send() for k in range(1, nz)])

    swap.wait_recv()

    def line(side, n):
        return at_e(y * nx + n) if side == 0 else at_e(n * nx + x)

    def line_of(side):
        return x if side == 0 else y

    def line_next(side, k):
        return lax.rem(line_of(side) + k, nx)

    def near_copy(side, zz, k):
        n = line_next(side, k)
        return remote(
            near_send.at[side, zz, n],
            near_recv.at[side, zz, line_of(side)],
            ps_sem.at[side, zz, k],
            pr_sem.at[side, zz, line_of(side)],
            line(side, n),
        )

    def farthest_last(k):
        return k + lax.div(k, 2) * (5 - 2 * k) if nz == 4 else k

    def project(k):
        zz = z_next(farthest_last(k))

        @pl.when(k > 0)
        def _():
            remote(
                mixed_v.at[zz], mixed_v.at[zz], ms_sem.at[0], mr_sem.at[zz], partner
            ).wait_recv()

        for side in range(2):
            part = jnp.dot(mixed_v[zz], w_v[side], preferred_element_type=F32)
            part = part.reshape(nx, nx, mine, block)
            if side == 0:
                part = jnp.stack(
                    [
                        jnp.concatenate([part[b, a] for b in range(nx)], axis=0)
                        for a in range(nx)
                    ]
                )
            near_send[side, zz] = part.reshape(nx, nx * mine, block).astype(BF16)
            for n in range(1, nx):
                near_copy(side, zz, n).start()
            near_recv[side, zz, line_of(side)] = near_send[side, zz, line_of(side)]

    sent.append(
        lambda: loop(
            nz,
            lambda zz: [
                near_copy(side, zz, n).wait_send() for side in range(2) for n in range(1, nx)
            ],
        )
    )

    def far_line(side, zz, n):
        if side == 0:
            return (zz * 2 + c, n * nx + x)
        return (zz * 2 + c, y * nx + n)

    def far_copy(side, zz, k):
        n = line_next(1 - side, k)
        return remote(
            far_send.at[side, zz, n],
            far_recv.at[side, z, line_of(1 - side)],
            zs_sem.at[side, zz, k],
            zr_sem.at[side, z, line_of(1 - side)],
            far_line(side, zz, n),
        )

    def far_out(k):
        zz = z_next(farthest_last(k))
        for side in range(2):
            for n in range(1, nx):
                m = line_next(side, n)
                remote(
                    near_send.at[side, zz, m],
                    near_recv.at[side, zz, m],
                    ps_sem.at[side, zz, 0],
                    pr_sem.at[side, zz, m],
                    partner,
                ).wait_recv()
            part = near_recv[side, zz, 0].astype(F32)
            for n in range(1, nx):
                part = part + near_recv[side, zz, n].astype(F32)
            part = part.reshape(nx, mine, block)
            part = jnp.concatenate([part[:, :, : block // 2], part[:, :, block // 2 :]], axis=1)
            far_send[side, zz] = part.astype(BF16)

            @pl.when(k == 0)
            def _():
                me = line_of(1 - side)
                far_recv[side, zz, me] = far_send[side, zz, me]

            @pl.when(k > 0)
            def _():
                far_copy(side, zz, 0).start()

            for n in range(1, nx):
                far_copy(side, zz, n).start()

    project(0)
    far_out(0)
    loop(nz - 1, lambda k: project(k + 1))
    loop(nz - 1, lambda k: far_out(k + 1))

    def drain_far():
        for side in range(2):
            for k in range(nz):
                for n in range(0 if k else 1, nx):
                    far_copy(side, z_next(k), n).wait_send()

    sent.append(drain_far)

    small[7].wait()
    small[8].wait()
    wide = width // parts
    hold = parts // 2
    pack = hold * CAP
    stacked = hold * mine
    places = nexp * pack
    lanes = lax.broadcasted_iota(jnp.int32, (mine, 128), 1)
    square = lax.broadcasted_iota(jnp.int32, (mine, mine), 0) == lax.broadcasted_iota(
        jnp.int32, (mine, mine), 1
    )
    earlier = (
        lax.broadcasted_iota(jnp.int32, (mine, mine), 0)
        > lax.broadcasted_iota(jnp.int32, (mine, mine), 1)
    ).astype(F32)
    column = lax.broadcasted_iota(jnp.int32, (stacked, places), 1)
    row = lax.broadcasted_iota(jnp.int32, (stacked, places), 0)
    column_slot = lax.div(column, pack) * CAP + lax.rem(column, CAP)
    same_part = lax.rem(lax.div(column, CAP), hold) == lax.div(row, mine)

    def column_of(values):
        return jnp.sum(jnp.where(square, values, 0.0), axis=1, keepdims=True)

    def tables(zz):
        meta = metas[zz]
        idents = [column_of(meta[n : n + 1, 0:mine]).astype(jnp.int32) for n in range(2)]
        hots = [(lanes == ident).astype(F32) for ident in idents]
        before = jnp.dot(earlier, hots[0] + hots[1], preferred_element_type=F32)
        table = jnp.zeros((stacked, places), F32)
        gated = jnp.zeros((stacked, places), F32)
        for n in range(2):
            rank = jnp.sum(before * hots[n], axis=1, keepdims=True).astype(jnp.int32)
            slot = jnp.concatenate([idents[n] * CAP + rank] * hold, axis=0)
            taken = jnp.where(same_part & (column_slot == slot), 1.0, 0.0)
            weight = column_of(meta[n + 2 : n + 3, 0:mine])
            table = table + taken
            gated = gated + taken * jnp.concatenate([weight] * hold, axis=0)
        gated_v[zz] = gated.astype(BF16)
        table_v[zz] = table.T.astype(BF16)

    tables(z)

    def other_tables(k):
        zz = z_next(k + 1)
        remote(meta_v, metas.at[zz], mt_sem.at[0, 0], mt_sem.at[1, zz], partner).wait_recv()
        tables(zz)

    loop(nz - 1, other_tables)

    source = lax.broadcasted_iota(jnp.int32, (places, places), 1)
    target = lax.broadcasted_iota(jnp.int32, (places, places), 0)

    def by_part(index):
        return (
            lax.rem(lax.div(index, CAP), hold) * slots
            + lax.div(index, pack) * CAP
            + lax.rem(index, CAP)
        )

    order_v[0] = (by_part(source) == target).astype(F32).astype(BF16)
    order_v[1] = (by_part(target) == source).astype(F32).astype(BF16)

    def stack(wide_rows):
        return jnp.concatenate(
            [wide_rows[:, k * wide : (k + 1) * wide] for k in range(parts)], axis=0
        )

    res = stack(res_v[...].astype(F32))
    gain = stack(jnp.broadcast_to(gain_v[...], (mine, width)))
    for side in range(2):
        for k in range(nz):
            for n in range(0 if k else 1, nx):
                zz, m = z_next(k), line_next(1 - side, n)
                remote(
                    far_send.at[side, zz, m],
                    far_recv.at[side, zz, m],
                    zs_sem.at[side, zz, 0],
                    zr_sem.at[side, zz, m],
                    partner,
                ).wait_recv()
    summed_parts = []
    for zz in range(nz):
        for side in range(2):
            part = far_recv[side, zz, 0].astype(F32)
            for n in range(1, nx):
                part = part + far_recv[side, zz, n].astype(F32)
            summed_parts.append(part)
    stream = (res + jnp.concatenate(summed_parts, axis=0)).astype(BF16).astype(F32)
    stream_v[...] = stream
    squares = jnp.sum(stream * stream, axis=1, keepdims=True).reshape(parts, mine, 1)
    scale = lax.rsqrt(jnp.sum(squares, axis=0) / width + EPSILON)
    normed = (stream * jnp.concatenate([scale] * parts, axis=0) * gain).astype(BF16)

    nrows[z] = normed[stacked:]

    def norm_copy(k):
        return remote(nrows.at[z], nrows.at[z], ns_sem.at[k], nr_sem.at[z], at_z(z_next(k)))

    for k in range(1, nz):
        norm_copy(k).start()
    sent.append(lambda: [norm_copy(k).wait_send() for k in range(1, nz)])

    def slotted(zz, rows):
        return (
            jnp.dot(table_v[zz], rows, preferred_element_type=F32)
            .astype(BF16)
            .reshape(nexp, pack, wide)
        )

    def left_copy(k):
        e = e_next(k)
        return remote(lsend.at[e], lrecv.at[j], ls_sem.at[k], lr_sem.at[j], at_e(e))

    lsend[...] = slotted(z, normed[:stacked])
    loop(nexp - 1, lambda k: left_copy(k + 1).start())
    lrecv[j] = lsend[j]
    sent.append(lambda: loop(nexp - 1, lambda k: left_copy(k + 1).wait_send()))

    def right_copy(k, first):
        e = e_next(k)
        which = pl.ds(0, 1) if first else pl.ds(1, nz - 1)
        n = 0 if first else 1
        return remote(
            qsend.at[e, which],
            qrecv.at[j, which],
            qs_sem.at[n, k],
            qr_sem.at[n, j],
            at_e(e),
        )

    qsend[:, 0] = slotted(z, normed[stacked:])
    loop(nexp - 1, lambda k: right_copy(k + 1, True).start())

    def right_slots(k):
        zz = z_next(k + 1)
        remote(nrows.at[zz], nrows.at[zz], ns_sem.at[0], nr_sem.at[zz], partner).wait_recv()
        qsend[:, k + 1] = slotted(zz, nrows[zz])

    loop(nz - 1, right_slots)
    loop(nexp - 1, lambda k: right_copy(k + 1, False).start())
    qrecv[j] = qsend[j]
    sent.append(
        lambda: loop(
            nexp - 1,
            lambda k: [right_copy(k + 1, first).wait_send() for first in (True, False)],
        )
    )

    def left_arrive(k):
        e = e_next(k + 1)
        remote(lsend.at[e], lrecv.at[e], ls_sem.at[0], lr_sem.at[e], partner).wait_recv()

    def rows_part(zz):
        return pl.ds(pl.multiple_of(zz * slots, slots), slots)

    def arranged(rows):
        return (
            jnp.dot(order_v[0], rows.reshape(places, wide), preferred_element_type=F32)
            .astype(BF16)
            .reshape(hold, slots, wide)
        )

    def rows_copy(g, n):
        here = rows_v.at[pl.ds(g * group, group), rows_part(z)]
        return remote(here, here, xs_sem.at[g, n], xr_sem.at[g, z], at_z(z_next(n)))

    def forward_copy(g, zz):
        return remote(
            rows_v.at[pl.ds(g * group, group), rows_part(zz)],
            rows_v.at[pl.ds(g * group, group), pl.ds(pl.multiple_of(half + zz * slots, slots), slots)],
            fs_sem.at[g, zz],
            fr_sem.at[g, zz],
            partner,
        )

    def right_forward(g):
        at = pl.ds(hold + g * group, group)
        return remote(
            rows_v.at[at, pl.ds(0, half)],
            rows_v.at[at, pl.ds(half, half)],
            gs_sem.at[g],
            gr_sem.at[g],
            partner,
        )

    group = hold // 2
    loop(nexp - 1, left_arrive)
    rows_v[0:hold, rows_part(z), :] = arranged(lrecv[...])
    for g in range(2):
        for n in range(1, nz):
            rows_copy(g, n).start()
        forward_copy(g, z).start()

    def right_arrive(n):
        which = pl.ds(0, 1) if n == 0 else pl.ds(1, nz - 1)

        def one(k):
            e = e_next(k + 1)
            remote(
                qsend.at[e, which], qrecv.at[e, which], qs_sem.at[n, 0], qr_sem.at[n, e], partner
            ).wait_recv()

        loop(nexp - 1, one)

    def right_rows(k):
        rows_v[hold:parts, rows_part(z_next(k)), :] = arranged(qrecv[:, k])

    right_arrive(0)
    right_rows(0)
    for g in range(2):
        for n in range(1, nz):
            zz = z_next(farthest_last(n))
            there = rows_v.at[pl.ds(g * group, group), rows_part(zz)]
            remote(there, there, xs_sem.at[g, 0], xr_sem.at[g, zz], partner).wait_recv()
            forward_copy(g, zz).start()
    right_arrive(1)
    loop(nz - 1, lambda k: right_rows(k + 1))
    for g in range(2):
        right_forward(g).start()

    def drain_rows():
        for g in range(2):
            right_forward(g).wait_send()
            for n in range(1, nz):
                rows_copy(g, n).wait_send()
            for zz in range(nz):
                forward_copy(g, zz).wait_send()

    sent.append(drain_rows)

    tile = 512 if hidden % 512 == 0 else hidden
    tiles = hidden // tile

    def tile_columns(n):
        return pl.ds(pl.multiple_of(n * tile, tile), tile)

    def half_product(first, columns):
        start = 0 if first else hold
        rows = jnp.concatenate([rows_v[start + k] for k in range(hold)], axis=1)
        weights = up_v[start * wide : (start + hold) * wide, columns]
        return jnp.dot(rows, weights, preferred_element_type=F32)

    loop(chunks, lambda k: up_copy(k).wait())
    for g in range(2):
        for zz in range(nz):
            forward_copy(g, zz).wait_recv()

    def lift_left(n):
        columns = tile_columns(n)
        acc_v[:, columns] = half_product(True, columns)

    loop(tiles, lift_left)
    for g in range(2):
        right_forward(g).wait_recv()

    def lift_right(n):
        columns = tile_columns(n)
        lifted = acc_v[:, columns] + half_product(False, columns)
        lifted_v[:, columns] = (lifted / (1.0 + jnp.exp(-lifted))).astype(BF16)

    loop(tiles, lift_right)
    loop(chunks, lambda k: down_copy(k).wait())

    halves = chunks // 2

    def step_of(k):
        return lax.rem(k + halves, chunks)

    def pair_copy(k):
        return remote(osend.at[k], orecv.at[k], os_sem.at[k], or_sem.at[k], partner)

    def lower(n):
        k = step_of(n)
        columns = pl.ds(pl.multiple_of(k * block, block), block)
        product = jnp.dot(lifted_v[...], down_v[:, columns], preferred_element_type=F32)
        okeep[k] = product[0:half]
        osend[k] = product[half : 2 * half].astype(BF16)
        pair_copy(k).start()

    def paired(k):
        pair_copy(k).wait_recv()
        return okeep[k] + orecv[k].astype(F32)

    def keep_right(n):
        both = paired(halves + n).astype(BF16)
        for q in range(2):
            rsum[2 * n + q] = both[:, q * wide : (q + 1) * wide].reshape(nz, slots, wide)

    lower(0)

    def right_step(n):
        lower(n + 1)
        keep_right(n)

    loop(halves, right_step)

    def unarranged(rows):
        return (
            jnp.dot(order_v[1], rows.reshape(places, wide), preferred_element_type=F32)
            .astype(BF16)
            .reshape(nexp, pack, wide)
        )

    def home_right_copy(k):
        e = e_next(k)
        return remote(qsend2.at[e], qrecv2.at[j], hq_sem.at[0, k], hq_sem.at[1, j], at_e(e))

    def home_right(k):
        qsend2[:, k] = unarranged(rsum[:, z_next(k)])

    loop(nz, home_right)
    loop(nexp - 1, lambda k: home_right_copy(k + 1).start())
    qrecv2[j] = qsend2[j]
    sent.append(lambda: loop(nexp - 1, lambda k: home_right_copy(k + 1).wait_send()))

    def back_copy(k, n):
        zz = z_next(n)
        return remote(
            rsend.at[k, zz], rrecv.at[k, z], rs_sem.at[k, n], rr_sem.at[k, z], at_z(zz)
        )

    def send_back(k):
        rsend[k] = paired(k).astype(BF16).reshape(nz, slots, block)
        for n in range(1, nz):
            back_copy(k, n).start()
        rrecv[k, z] = rsend[k, z]

    def left_step(n):
        lower(n + halves + 1)
        send_back(n)

    loop(halves - 1, left_step)
    send_back(halves - 1)

    def drain_back(k):
        for n in range(1, nz):
            back_copy(k, n).wait_send()

    sent.append(lambda: loop(halves, drain_back))
    sent.append(lambda: loop(chunks, lambda k: pair_copy(k).wait_send()))

    def back_arrive(k):
        for n in range(1, nz):
            zz = z_next(n)
            remote(
                rsend.at[k, zz], rrecv.at[k, zz], rs_sem.at[k, 0], rr_sem.at[k, zz], partner
            ).wait_recv()
        total = rrecv[k, 0].astype(F32)
        for zz in range(1, nz):
            total = total + rrecv[k, zz].astype(F32)
        for q in range(2):
            lsum[2 * k + q] = total[:, q * wide : (q + 1) * wide].astype(BF16)

    loop(halves, back_arrive)
    lsend2[...] = unarranged(lsum[...])

    def home_left_copy(k):
        e = e_next(k)
        return remote(lsend2.at[e], lrecv2.at[j], hl_sem.at[0, k], hl_sem.at[1, j], at_e(e))

    loop(nexp - 1, lambda k: home_left_copy(k + 1).start())
    lrecv2[j] = lsend2[j]
    sent.append(lambda: loop(nexp - 1, lambda k: home_left_copy(k + 1).wait_send()))

    def home_right_arrive(k):
        e = e_next(k + 1)
        remote(
            qsend2.at[e], qrecv2.at[e], hq_sem.at[0, 0], hq_sem.at[1, e], partner
        ).wait_recv()

    loop(nexp - 1, home_right_arrive)

    def weighed(zz, rows):
        return jnp.dot(gated_v[zz], rows.reshape(places, wide), preferred_element_type=F32)

    def token_copy(k):
        zz = z_next(k)
        return remote(csend.at[zz], crecv.at[z], cs_sem.at[0, k], cs_sem.at[1, z], at_z(zz))

    for n in range(1, nz):
        k = n + n // 2 * (5 - 2 * n) if nz == 4 else n
        zz = z_next(k)
        csend[zz] = weighed(zz, qrecv2[:, k]).astype(BF16)
        token_copy(k).start()
    crecv[z] = weighed(z, qrecv2[:, 0]).astype(BF16)
    sent.append(lambda: [token_copy(k).wait_send() for k in range(1, nz)])

    def home_left_arrive(k):
        e = e_next(k + 1)
        remote(
            lsend2.at[e], lrecv2.at[e], hl_sem.at[0, 0], hl_sem.at[1, e], partner
        ).wait_recv()

    def give(first, rows):
        for k in range(hold):
            at = (0 if first else hold) + k
            out_ref[:, at * wide : (at + 1) * wide] = rows[k * mine : (k + 1) * mine].astype(BF16)

    loop(nexp - 1, home_left_arrive)
    give(True, stream_v[0:stacked] + weighed(z, lrecv2[...]))
    for k in range(1, nz):
        zz = z_next(k)
        remote(
            csend.at[zz], crecv.at[zz], cs_sem.at[0, 0], cs_sem.at[1, zz], partner
        ).wait_recv()
    total = stream_v[stacked : 2 * stacked]
    for zz in range(nz):
        total = total + crecv[zz].astype(F32)
    give(False, total)

    for drain in sent:
        drain()


def shards(nctx, nexp, *arrays):
    (
        mixer_input,
        mixer_gate,
        step_size,
        write_coeffs,
        read_coeffs,
        decay_rates,
        skip_scale,
        out_weight,
        residual_in,
        norm_gain,
        expert_ids,
        gate_weights,
        up_weight,
        down_weight,
    ) = arrays
    tokens, channels = mixer_input.shape
    states = write_coeffs.shape[1]
    mine, width = residual_in.shape
    hidden = up_weight.shape[2]
    nz = nctx // 2
    nx = math.isqrt(nexp)
    block = width // nctx
    chunks = nctx
    slots = nexp * CAP
    parts = 2 * chunks
    wide = width // parts
    hold = parts // 2
    pack = hold * CAP
    stacked = hold * mine
    places = nexp * pack
    operands = (
        mixer_input,
        mixer_gate,
        step_size,
        write_coeffs.T,
        read_coeffs.T,
        decay_rates.T,
        skip_scale.reshape(1, channels),
        out_weight,
        residual_in,
        norm_gain.reshape(1, width),
        expert_ids.T,
        gate_weights.T,
        up_weight.reshape(width, hidden),
        down_weight.reshape(hidden, width),
    )
    dma = pltpu.SemaphoreType.DMA
    scratch = [
        pltpu.VMEM((tokens, channels), BF16),
        pltpu.VMEM((tokens, channels), BF16),
        pltpu.VMEM((tokens, channels), BF16),
        pltpu.VMEM((states, tokens), F32),
        pltpu.VMEM((states, tokens), F32),
        pltpu.VMEM((states, channels), F32),
        pltpu.VMEM((1, channels), F32),
        pltpu.VMEM((mine, width), BF16),
        pltpu.VMEM((1, width), F32),
        pltpu.VMEM((2, mine), jnp.int32),
        pltpu.VMEM((2, mine), BF16),
        pltpu.VMEM((tokens, states), F32),
        pltpu.VMEM((tokens, states), F32),
        pltpu.VMEM((width, hidden), BF16),
        pltpu.VMEM((hidden, width), BF16),
        pltpu.VMEM((2, channels, block), BF16),
        pltpu.VMEM((tokens, channels), F32),
        pltpu.VMEM((tokens, channels), F32),
        pltpu.VMEM((tokens, states, 128), F32),
        pltpu.VMEM((tokens, states, 128), F32),
        pltpu.VMEM((states, channels), F32),
        pltpu.VMEM((states, channels), F32),
        pltpu.VMEM((states, channels), BF16),
        pltpu.VMEM((nctx, states, channels), BF16),
        pltpu.VMEM((8, 128), F32),
        pltpu.VMEM((nctx, 8, 128), F32),
        pltpu.VMEM((8, 128), F32),
        pltpu.VMEM((nz, 8, 128), F32),
        pltpu.VMEM((nz, tokens, channels), BF16),
        pltpu.VMEM((2, nz, nx, nx * mine, block), BF16),
        pltpu.VMEM((2, nz, nx, nx * mine, block), BF16),
        pltpu.VMEM((2, nz, nx, 2 * mine, wide), BF16),
        pltpu.VMEM((2, nz, nx, 2 * mine, wide), BF16),
        pltpu.VMEM((parts * mine, wide), F32),
        pltpu.VMEM((nz, places, stacked), BF16),
        pltpu.VMEM((nz, stacked, places), BF16),
        pltpu.VMEM((2, places, places), BF16),
        pltpu.VMEM((nz, stacked, wide), BF16),
        pltpu.VMEM((nexp, pack, wide), BF16),
        pltpu.VMEM((nexp, pack, wide), BF16),
        pltpu.VMEM((nexp, nz, pack, wide), BF16),
        pltpu.VMEM((nexp, nz, pack, wide), BF16),
        pltpu.VMEM((parts, nctx * slots, wide), BF16),
        pltpu.VMEM((nctx * slots, hidden), F32),
        pltpu.VMEM((nctx * slots, hidden), BF16),
        pltpu.VMEM((chunks, nz * slots, block), BF16),
        pltpu.VMEM((chunks, nz * slots, block), BF16),
        pltpu.VMEM((chunks, nz * slots, block), F32),
        pltpu.VMEM((hold, nz, slots, wide), BF16),
        pltpu.VMEM((hold, slots, wide), BF16),
        pltpu.VMEM((hold // 2, nz, slots, block), BF16),
        pltpu.VMEM((hold // 2, nz, slots, block), BF16),
        pltpu.VMEM((nexp, nz, pack, wide), BF16),
        pltpu.VMEM((nexp, nz, pack, wide), BF16),
        pltpu.VMEM((nexp, pack, wide), BF16),
        pltpu.VMEM((nexp, pack, wide), BF16),
        pltpu.VMEM((nz, stacked, wide), BF16),
        pltpu.VMEM((nz, stacked, wide), BF16),
        dma((12,)),
        dma((2, chunks)),
        dma((2,)),
        dma((2, nctx)),
        dma((2, nctx)),
        dma((nz,)),
        dma((nz,)),
        dma((2, nz, nx)),
        dma((2, nz, nx)),
        dma((2, nz, nx)),
        dma((2, nz, nx)),
        dma((2, nz)),
        dma((nz,)),
        dma((nz,)),
        dma((nexp,)),
        dma((nexp,)),
        dma((2, nexp)),
        dma((2, nexp)),
        dma((2, nz)),
        dma((2, nz)),
        dma((2, nz)),
        dma((2, nz)),
        dma((2,)),
        dma((2,)),
        dma((chunks,)),
        dma((chunks,)),
        dma((hold // 2, nz)),
        dma((hold // 2, nz)),
        dma((2, nexp)),
        dma((2, nexp)),
        dma((2, nz)),
    ]
    return pl.pallas_call(
        functools.partial(kernel, nctx, nexp),
        out_shape=jax.ShapeDtypeStruct((mine, width), BF16),
        in_specs=[pl.BlockSpec(memory_space=pl.ANY)] * len(operands),
        out_specs=pl.BlockSpec(memory_space=pltpu.VMEM),
        scratch_shapes=scratch,
        compiler_params=pltpu.CompilerParams(
            collective_id=0, has_side_effects=True, vmem_limit_bytes=60 * 2**20
        ),
    )(*operands)


def solution(mesh):
    return jax.shard_map(
        functools.partial(shards, mesh.shape["ctx"], mesh.shape["exp"]),
        mesh=mesh,
        in_specs=(
            P("ctx", "exp"),
            P("ctx", "exp"),
            P("ctx", "exp"),
            P("ctx", None),
            P("ctx", None),
            P("exp", None),
            P("exp"),
            P("exp", "ctx"),
            P(("ctx", "exp"), None),
            P(),
            P(("ctx", "exp"), None),
            P(("ctx", "exp"), None),
            P("exp", None, "ctx"),
            P("exp", "ctx", None),
        ),
        out_specs=P(("ctx", "exp"), None),
        check_vma=False,
    )
```

time: 90.2 us -> 77.5 us (0.86)
  Pallas kernels: 88.6 us -> 75.9 us
    pallas_call x1, Pallas kernels: 88.6 us -> 75.9 us  [shards(): pl.pallas_call(functools.partial(kernel, nctx, nexp), out_shape=jax.Shape...]
where the time goes in v1:
time: 77.5 us; the launch traced here: 77.3 us
  Pallas kernels  75.9 us (98%)
  local copies, waits for them, and re-layouts  1.47 us (2%)
    pallas_call x1, Pallas kernels, shards(): pl.pallas_call(functools.partial(kernel, nctx, nexp), out_shape=jax.Shape...  75.9 us

profile of v1, /device:TPU:0, one launch (start us, length us, event | category | flops | bytes accessed | tf_op | source)
XLA Modules:
  0.0 77.3 jit_solution(15285010234449589574)
XLA Ops:
  0.0 75.9 %shard_map.136 = bf16[8,4096]{1,0:T(8,128)(2,1)} custom-call(bf16[128,512]{1,0:T(8,128)(2,1)} %x_hbm.1, bf16[128,512]{1,0:T(8,128)(2,1)} %gate_hbm.1, bf16[128,512]{1,0:T(8,128)(2,1)} %step_hbm.1, f32[16,128]{1,0:T(8,128)} %bitcast.13, f32[16,128]{1,0:T(8,128)} %bitcast.14, f32[16,512]{1,0:T(8,128)} %bitcast.11, f32[1,512]{1,0:T(1,128)} %bitcast.15, ...), custom_call_target="tpu_custom_call" | custom-call | tf_op jit(solution)/shard_map/pallas_call | solution.py:1030
  75.9 1.5 %copy.16 = bf16[8,4096]{1,0:T(8,128)(2,1)} copy(bf16[8,4096]{1,0:T(8,128)(2,1)} %shard_map.136) | data formatting | bytes 131072

commit v2 on v1

--- a/solution.py
+++ b/solution.py
@@ -91,6 +91,7 @@
     table_v,
     gated_v,
     order_v,
+    slot_v,
     nrows,
     lsend,
     lrecv,
@@ -277,6 +278,38 @@
     meta_v[0:2, 0:mine] = ids_v[...].astype(F32)
     meta_v[2:4, 0:mine] = pairgate_v[...].astype(F32)
 
+    wide = width // parts
+    hold = parts // 2
+    pack = hold * CAP
+    stacked = hold * mine
+    places = nexp * pack
+    lanes = lax.broadcasted_iota(jnp.int32, (mine, 128), 1)
+    square = lax.broadcasted_iota(jnp.int32, (mine, mine), 0) == lax.broadcasted_iota(
+        jnp.int32, (mine, mine), 1
+    )
+    earlier = (
+        lax.broadcasted_iota(jnp.int32, (mine, mine), 0)
+        > lax.broadcasted_iota(jnp.int32, (mine, mine), 1)
+    ).astype(F32)
+    column = lax.broadcasted_iota(jnp.int32, (stacked, places), 1)
+    row = lax.broadcasted_iota(jnp.int32, (stacked, places), 0)
+    column_slot = lax.div(column, pack) * CAP + lax.rem(column, CAP)
+    same_part = lax.rem(lax.div(column, CAP), hold) == lax.div(row, mine)
+    slot_v[...] = jnp.where(same_part, column_slot, -1)
+
+    source = lax.broadcasted_iota(jnp.int32, (places, places), 1)
+    target = lax.broadcasted_iota(jnp.int32, (places, places), 0)
+
+    def by_part(index):
+        return (
+            lax.rem(lax.div(index, CAP), hold) * slots
+            + lax.div(index, pack) * CAP
+            + lax.rem(index, CAP)
+        )
+
+    order_v[0] = (by_part(source) == target).astype(F32).astype(BF16)
+    order_v[1] = (by_part(target) == source).astype(F32).astype(BF16)
+
     pl.semaphore_wait(barrier, nctx - 1 + 2 * (nx - 1))
 
     def state_copies(k):
@@ -346,16 +379,28 @@
         mixed_v[z, part, :] = (readout * (gate / (1.0 + jnp.exp(-gate)))).astype(BF16)
         return h
 
-    lax.fori_loop(0, tokens // STEPS, second, h_v[...])
-
-    def mixed_copy(k):
-        return remote(
-            mixed_v.at[z], mixed_v.at[z], ms_sem.at[k], mr_sem.at[z], at_z(z_next(k))
-        )
-
-    for k in range(1, nz):
-        mixed_copy(k).start()
-    sent.append(lambda: [mixed_copy(k).wait_send() for k in range(1, nz)])
+    reach = (1, nz - 1) if nz > 2 else (1,)
+    beyond = tuple(range(2, nz - 1))
+
+    def mixed_copy(n, k):
+        part = mixed_v.at[z, n * (tokens // 2) : (n + 1) * (tokens // 2)]
+        return remote(part, part, ms_sem.at[n, k], mr_sem.at[n, z], at_z(z_next(k)))
+
+    def mixed_arrive(zz):
+        for n in range(2):
+            part = mixed_v.at[zz, n * (tokens // 2) : (n + 1) * (tokens // 2)]
+            remote(part, part, ms_sem.at[n, 0], mr_sem.at[n, zz], partner).wait_recv()
+
+    turns = tokens // STEPS // 2
+    h = h_v[...]
+    for n in range(2):
+        h = lax.fori_loop(n * turns, (n + 1) * turns, second, h)
+        for k in reach:
+            mixed_copy(n, k).start()
+    for n in range(2):
+        for k in beyond:
+            mixed_copy(n, k).start()
+    sent.append(lambda: [mixed_copy(n, k).wait_send() for k in reach + beyond for n in range(2)])
 
     swap.wait_recv()
 
@@ -386,9 +431,7 @@
 
         @pl.when(k > 0)
         def _():
-            remote(
-                mixed_v.at[zz], mixed_v.at[zz], ms_sem.at[0], mr_sem.at[zz], partner
-            ).wait_recv()
+            mixed_arrive(zz)
 
         for side in range(2):
             part = jnp.dot(mixed_v[zz], w_v[side], preferred_element_type=F32)
@@ -461,38 +504,6 @@
                 far_copy(side, zz, n).start()
 
     project(0)
-    far_out(0)
-    loop(nz - 1, lambda k: project(k + 1))
-    loop(nz - 1, lambda k: far_out(k + 1))
-
-    def drain_far():
-        for side in range(2):
-            for k in range(nz):
-                for n in range(0 if k else 1, nx):
-                    far_copy(side, z_next(k), n).wait_send()
-
-    sent.append(drain_far)
-
-    small[7].wait()
-    small[8].wait()
-    wide = width // parts
-    hold = parts // 2
-    pack = hold * CAP
-    stacked = hold * mine
-    places = nexp * pack
-    lanes = lax.broadcasted_iota(jnp.int32, (mine, 128), 1)
-    square = lax.broadcasted_iota(jnp.int32, (mine, mine), 0) == lax.broadcasted_iota(
-        jnp.int32, (mine, mine), 1
-    )
-    earlier = (
-        lax.broadcasted_iota(jnp.int32, (mine, mine), 0)
-        > lax.broadcasted_iota(jnp.int32, (mine, mine), 1)
-    ).astype(F32)
-    column = lax.broadcasted_iota(jnp.int32, (stacked, places), 1)
-    row = lax.broadcasted_iota(jnp.int32, (stacked, places), 0)
-    column_slot = lax.div(column, pack) * CAP + lax.rem(column, CAP)
-    same_part = lax.rem(lax.div(column, CAP), hold) == lax.div(row, mine)
-
     def column_of(values):
         return jnp.sum(jnp.where(square, values, 0.0), axis=1, keepdims=True)
 
@@ -506,7 +517,7 @@
         for n in range(2):
             rank = jnp.sum(before * hots[n], axis=1, keepdims=True).astype(jnp.int32)
             slot = jnp.concatenate([idents[n] * CAP + rank] * hold, axis=0)
-            taken = jnp.where(same_part & (column_slot == slot), 1.0, 0.0)
+            taken = jnp.where(slot_v[...] == slot, 1.0, 0.0)
             weight = column_of(meta[n + 2 : n + 3, 0:mine])
             table = table + taken
             gated = gated + taken * jnp.concatenate([weight] * hold, axis=0)
@@ -521,25 +532,25 @@
         tables(zz)
 
     loop(nz - 1, other_tables)
-
-    source = lax.broadcasted_iota(jnp.int32, (places, places), 1)
-    target = lax.broadcasted_iota(jnp.int32, (places, places), 0)
-
-    def by_part(index):
-        return (
-            lax.rem(lax.div(index, CAP), hold) * slots
-            + lax.div(index, pack) * CAP
-            + lax.rem(index, CAP)
-        )
-
-    order_v[0] = (by_part(source) == target).astype(F32).astype(BF16)
-    order_v[1] = (by_part(target) == source).astype(F32).astype(BF16)
+    far_out(0)
+    loop(nz - 1, lambda k: project(k + 1))
+    loop(nz - 1, lambda k: far_out(k + 1))
+
+    def drain_far():
+        for side in range(2):
+            for k in range(nz):
+                for n in range(0 if k else 1, nx):
+                    far_copy(side, z_next(k), n).wait_send()
+
+    sent.append(drain_far)
 
     def stack(wide_rows):
         return jnp.concatenate(
             [wide_rows[:, k * wide : (k + 1) * wide] for k in range(parts)], axis=0
         )
 
+    small[7].wait()
+    small[8].wait()
     res = stack(res_v[...].astype(F32))
     gain = stack(jnp.broadcast_to(gain_v[...], (mine, width)))
     for side in range(2):
@@ -591,35 +602,22 @@
     lrecv[j] = lsend[j]
     sent.append(lambda: loop(nexp - 1, lambda k: left_copy(k + 1).wait_send()))
 
-    def right_copy(k, first):
+    def right_copy(k):
         e = e_next(k)
-        which = pl.ds(0, 1) if first else pl.ds(1, nz - 1)
-        n = 0 if first else 1
-        return remote(
-            qsend.at[e, which],
-            qrecv.at[j, which],
-            qs_sem.at[n, k],
-            qr_sem.at[n, j],
-            at_e(e),
-        )
+        return remote(qsend.at[e], qrecv.at[j], qs_sem.at[0, k], qr_sem.at[0, j], at_e(e))
 
     qsend[:, 0] = slotted(z, normed[stacked:])
-    loop(nexp - 1, lambda k: right_copy(k + 1, True).start())
-
-    def right_slots(k):
-        zz = z_next(k + 1)
-        remote(nrows.at[zz], nrows.at[zz], ns_sem.at[0], nr_sem.at[zz], partner).wait_recv()
-        qsend[:, k + 1] = slotted(zz, nrows[zz])
-
-    loop(nz - 1, right_slots)
-    loop(nexp - 1, lambda k: right_copy(k + 1, False).start())
-    qrecv[j] = qsend[j]
-    sent.append(
-        lambda: loop(
-            nexp - 1,
-            lambda k: [right_copy(k + 1, first).wait_send() for first in (True, False)],
-        )
-    )
+
+    def right_out():
+        def right_slots(k):
+            zz = z_next(k + 1)
+            remote(nrows.at[zz], nrows.at[zz], ns_sem.at[0], nr_sem.at[zz], partner).wait_recv()
+            qsend[:, k + 1] = slotted(zz, nrows[zz])
+
+        loop(nz - 1, right_slots)
+        loop(nexp - 1, lambda k: right_copy(k + 1).start())
+        qrecv[j] = qsend[j]
+        sent.append(lambda: loop(nexp - 1, lambda k: right_copy(k + 1).wait_send()))
 
     def left_arrive(k):
         e = e_next(k + 1)
@@ -666,30 +664,52 @@
             rows_copy(g, n).start()
         forward_copy(g, z).start()
 
-    def right_arrive(n):
-        which = pl.ds(0, 1) if n == 0 else pl.ds(1, nz - 1)
-
+    right_out()
+
+    def right_arrive():
         def one(k):
             e = e_next(k + 1)
-            remote(
-                qsend.at[e, which], qrecv.at[e, which], qs_sem.at[n, 0], qr_sem.at[n, e], partner
-            ).wait_recv()
+            remote(qsend.at[e], qrecv.at[e], qs_sem.at[0, 0], qr_sem.at[0, e], partner).wait_recv()
 
         loop(nexp - 1, one)
 
     def right_rows(k):
         rows_v[hold:parts, rows_part(z_next(k)), :] = arranged(qrecv[:, k])
 
-    right_arrive(0)
-    right_rows(0)
-    for g in range(2):
+    tile = 512 if hidden % 512 == 0 else hidden
+    tiles = hidden // tile
+
+    def tile_columns(n):
+        return pl.ds(pl.multiple_of(n * tile, tile), tile)
+
+    def product(start, count, columns):
+        rows = jnp.concatenate([rows_v[start + k] for k in range(count)], axis=1)
+        weights = up_v[start * wide : (start + count) * wide, columns]
+        return jnp.dot(rows, weights, preferred_element_type=F32)
+
+    def group_arrive(g):
         for n in range(1, nz):
             zz = z_next(farthest_last(n))
             there = rows_v.at[pl.ds(g * group, group), rows_part(zz)]
             remote(there, there, xs_sem.at[g, 0], xr_sem.at[g, zz], partner).wait_recv()
             forward_copy(g, zz).start()
-    right_arrive(1)
-    loop(nz - 1, lambda k: right_rows(k + 1))
+
+    def group_forwarded(g):
+        for zz in range(nz):
+            forward_copy(g, zz).wait_recv()
+
+    group_arrive(0)
+    loop(chunks, lambda k: up_copy(k).wait())
+    group_forwarded(0)
+
+    def lift_first(n):
+        columns = tile_columns(n)
+        acc_v[:, columns] = product(0, group, columns)
+
+    loop(tiles, lift_first)
+    group_arrive(1)
+    right_arrive()
+    loop(nz, right_rows)
     for g in range(2):
         right_forward(g).start()
 
@@ -702,35 +722,19 @@
                 forward_copy(g, zz).wait_send()
 
     sent.append(drain_rows)
-
-    tile = 512 if hidden % 512 == 0 else hidden
-    tiles = hidden // tile
-
-    def tile_columns(n):
-        return pl.ds(pl.multiple_of(n * tile, tile), tile)
-
-    def half_product(first, columns):
-        start = 0 if first else hold
-        rows = jnp.concatenate([rows_v[start + k] for k in range(hold)], axis=1)
-        weights = up_v[start * wide : (start + hold) * wide, columns]
-        return jnp.dot(rows, weights, preferred_element_type=F32)
-
-    loop(chunks, lambda k: up_copy(k).wait())
-    for g in range(2):
-        for zz in range(nz):
-            forward_copy(g, zz).wait_recv()
-
-    def lift_left(n):
+    group_forwarded(1)
+
+    def lift_second(n):
         columns = tile_columns(n)
-        acc_v[:, columns] = half_product(True, columns)
-
-    loop(tiles, lift_left)
+        acc_v[:, columns] += product(group, group, columns)
+
+    loop(tiles, lift_second)
     for g in range(2):
         right_forward(g).wait_recv()
 
     def lift_right(n):
         columns = tile_columns(n)
-        lifted = acc_v[:, columns] + half_product(False, columns)
+        lifted = acc_v[:, columns] + product(hold, hold, columns)
         lifted_v[:, columns] = (lifted / (1.0 + jnp.exp(-lifted))).astype(BF16)
 
     loop(tiles, lift_right)
@@ -761,13 +765,26 @@
         for q in range(2):
             rsum[2 * n + q] = both[:, q * wide : (q + 1) * wide].reshape(nz, slots, wide)
 
-    lower(0)
-
-    def right_step(n):
-        lower(n + 1)
-        keep_right(n)
-
-    loop(halves, right_step)
+    def back_copy(k, n):
+        zz = z_next(n)
+        return remote(
+            rsend.at[k, zz], rrecv.at[k, z], rs_sem.at[k, n], rr_sem.at[k, z], at_z(zz)
+        )
+
+    def send_back(k):
+        rsend[k] = paired(k).astype(BF16).reshape(nz, slots, block)
+        for n in range(1, nz):
+            back_copy(k, n).start()
+        rrecv[k, z] = rsend[k, z]
+
+    ahead = halves // 2
+    loop(ahead, lambda n: lower(halves + n))
+    for n in range(halves):
+        lower(n)
+    loop(ahead, send_back)
+    loop(halves - 1, keep_right)
+    lower(halves + ahead)
+    keep_right(halves - 1)
 
     def unarranged(rows):
         return (
@@ -776,36 +793,35 @@
             .reshape(nexp, pack, wide)
         )
 
-    def home_right_copy(k):
+    def home_right_copy(k, first):
         e = e_next(k)
-        return remote(qsend2.at[e], qrecv2.at[j], hq_sem.at[0, k], hq_sem.at[1, j], at_e(e))
+        which = pl.ds(1, nz - 1) if first else pl.ds(0, 1)
+        n = 0 if first else 1
+        return remote(
+            qsend2.at[e, which],
+            qrecv2.at[j, which],
+            hq_sem.at[0, n, k],
+            hq_sem.at[1, n, j],
+            at_e(e),
+        )
 
     def home_right(k):
         qsend2[:, k] = unarranged(rsum[:, z_next(k)])
 
-    loop(nz, home_right)
-    loop(nexp - 1, lambda k: home_right_copy(k + 1).start())
+    loop(nz - 1, lambda k: home_right(k + 1))
+    loop(nexp - 1, lambda k: home_right_copy(k + 1, True).start())
+    home_right(0)
+    loop(nexp - 1, lambda k: home_right_copy(k + 1, False).start())
     qrecv2[j] = qsend2[j]
-    sent.append(lambda: loop(nexp - 1, lambda k: home_right_copy(k + 1).wait_send()))
-
-    def back_copy(k, n):
-        zz = z_next(n)
-        return remote(
-            rsend.at[k, zz], rrecv.at[k, z], rs_sem.at[k, n], rr_sem.at[k, z], at_z(zz)
-        )
-
-    def send_back(k):
-        rsend[k] = paired(k).astype(BF16).reshape(nz, slots, block)
-        for n in range(1, nz):
-            back_copy(k, n).start()
-        rrecv[k, z] = rsend[k, z]
-
-    def left_step(n):
-        lower(n + halves + 1)
-        send_back(n)
-
-    loop(halves - 1, left_step)
-    send_back(halves - 1)
+    sent.append(
+        lambda: loop(
+            nexp - 1,
+            lambda k: [home_right_copy(k + 1, first).wait_send() for first in (True, False)],
+        )
+    )
+
+    loop(halves - ahead - 1, lambda n: lower(n + halves + ahead + 1))
+    loop(halves - ahead, lambda n: send_back(n + ahead))
 
     def drain_back(k):
         for n in range(1, nz):
@@ -837,13 +853,22 @@
     lrecv2[j] = lsend2[j]
     sent.append(lambda: loop(nexp - 1, lambda k: home_left_copy(k + 1).wait_send()))
 
-    def home_right_arrive(k):
-        e = e_next(k + 1)
-        remote(
-            qsend2.at[e], qrecv2.at[e], hq_sem.at[0, 0], hq_sem.at[1, e], partner
-        ).wait_recv()
-
-    loop(nexp - 1, home_right_arrive)
+    def home_right_arrive(n):
+        which = pl.ds(1, nz - 1) if n == 0 else pl.ds(0, 1)
+
+        def one(k):
+            e = e_next(k + 1)
+            remote(
+                qsend2.at[e, which],
+                qrecv2.at[e, which],
+                hq_sem.at[0, n, 0],
+                hq_sem.at[1, n, e],
+                partner,
+            ).wait_recv()
+
+        loop(nexp - 1, one)
+
+    home_right_arrive(0)
 
     def weighed(zz, rows):
         return jnp.dot(gated_v[zz], rows.reshape(places, wide), preferred_element_type=F32)
@@ -857,6 +882,7 @@
         zz = z_next(k)
         csend[zz] = weighed(zz, qrecv2[:, k]).astype(BF16)
         token_copy(k).start()
+    home_right_arrive(1)
     crecv[z] = weighed(z, qrecv2[:, 0]).astype(BF16)
     sent.append(lambda: [token_copy(k).wait_send() for k in range(1, nz)])
 
@@ -974,6 +1000,7 @@
         pltpu.VMEM((nz, places, stacked), BF16),
         pltpu.VMEM((nz, stacked, places), BF16),
         pltpu.VMEM((2, places, places), BF16),
+        pltpu.VMEM((stacked, places), jnp.int32),
         pltpu.VMEM((nz, stacked, wide), BF16),
         pltpu.VMEM((nexp, pack, wide), BF16),
         pltpu.VMEM((nexp, pack, wide), BF16),
@@ -1000,8 +1027,8 @@
         dma((2,)),
         dma((2, nctx)),
         dma((2, nctx)),
-        dma((nz,)),
-        dma((nz,)),
+        dma((2, nz)),
+        dma((2, nz)),
         dma((2, nz, nx)),
         dma((2, nz, nx)),
         dma((2, nz, nx)),
@@ -1023,7 +1050,7 @@
         dma((chunks,)),
         dma((hold // 2, nz)),
         dma((hold // 2, nz)),
-        dma((2, nexp)),
+        dma((2, 2, nexp)),
         dma((2, nexp)),
         dma((2, nz)),
     ]

time: 77.5 us -> 72.5 us (0.935)
  Pallas kernels: 75.9 us -> 70.9 us
    pallas_call x1, Pallas kernels: 75.9 us -> 70.9 us  [shards(): pl.pallas_call(functools.partial(kernel, nctx, nexp), out_shape=jax.Shape...]
where the time goes in v2:
time: 72.5 us; the launch traced here: 72.4 us
  Pallas kernels  70.9 us (98%)
  local copies, waits for them, and re-layouts  1.47 us (2%)
    pallas_call x1, Pallas kernels, shards(): pl.pallas_call(functools.partial(kernel, nctx, nexp), out_shape=jax.Shape...  70.9 us
    unnamed x1, local copies, waits for them, and re-layouts  1.47 us

profile of v2, /device:TPU:0, one launch (start us, length us, event | category | flops | bytes accessed | tf_op | source)
XLA Modules:
  0.0 72.4 jit_solution(3879625479681389201)
XLA Ops:
  0.0 70.9 %shard_map.136 = bf16[8,4096]{1,0:T(8,128)(2,1)} custom-call(bf16[128,512]{1,0:T(8,128)(2,1)} %x_hbm.1, bf16[128,512]{1,0:T(8,128)(2,1)} %gate_hbm.1, bf16[128,512]{1,0:T(8,128)(2,1)} %step_hbm.1, f32[16,128]{1,0:T(8,128)} %bitcast.13, f32[16,128]{1,0:T(8,128)} %bitcast.14, f32[16,512]{1,0:T(8,128)} %bitcast.11, f32[1,512]{1,0:T(1,128)} %bitcast.15, ...), custom_call_target="tpu_custom_call" | custom-call | tf_op jit(solution)/shard_map/pallas_call | solution.py:1057
  70.9 1.5 %copy.16 = bf16[8,4096]{1,0:T(8,128)(2,1)} copy(bf16[8,4096]{1,0:T(8,128)(2,1)} %shard_map.136) | data formatting | bytes 131072

commit v3 on v2

--- a/solution.py
+++ b/solution.py
@@ -34,6 +34,11 @@
         return carry
 
     lax.fori_loop(0, count, step, 0)
+
+
+def burst(count, body):
+    for k in range(count):
+        body(k)
 
 
 def kernel(
@@ -175,6 +180,18 @@
     def e_next(k):
         return lax.rem(j + k, nexp)
 
+    barrier = pltpu.get_barrier_semaphore()
+
+    def greet_ctx(k):
+        pl.semaphore_signal(
+            barrier, inc=1, device_id=(lax.rem(i + k + 1, nctx), j), device_id_type=MESH
+        )
+
+    loop(nctx - 1, greet_ctx)
+    for k in range(1, nx):
+        for e in (y * nx + lax.rem(x + k, nx), lax.rem(y + k, nx) * nx + x):
+            pl.semaphore_signal(barrier, inc=1, device_id=at_e(e), device_id_type=MESH)
+
     small = [
         (write_hbm, write_v),
         (read_hbm, read_v),
@@ -194,18 +211,6 @@
     ]
     for copy in small:
         copy.start()
-
-    barrier = pltpu.get_barrier_semaphore()
-
-    def greet_ctx(k):
-        pl.semaphore_signal(
-            barrier, inc=1, device_id=(lax.rem(i + k + 1, nctx), j), device_id_type=MESH
-        )
-
-    loop(nctx - 1, greet_ctx)
-    for k in range(1, nx):
-        for e in (y * nx + lax.rem(x + k, nx), lax.rem(y + k, nx) * nx + x):
-            pl.semaphore_signal(barrier, inc=1, device_id=at_e(e), device_id_type=MESH)
 
     def up_copy(k):
         part = pl.ds(pl.multiple_of(k * block, block), block)
@@ -598,7 +603,7 @@
         return remote(lsend.at[e], lrecv.at[j], ls_sem.at[k], lr_sem.at[j], at_e(e))
 
     lsend[...] = slotted(z, normed[:stacked])
-    loop(nexp - 1, lambda k: left_copy(k + 1).start())
+    burst(nexp - 1, lambda k: left_copy(k + 1).start())
     lrecv[j] = lsend[j]
     sent.append(lambda: loop(nexp - 1, lambda k: left_copy(k + 1).wait_send()))
 
@@ -614,8 +619,8 @@
             remote(nrows.at[zz], nrows.at[zz], ns_sem.at[0], nr_sem.at[zz], partner).wait_recv()
             qsend[:, k + 1] = slotted(zz, nrows[zz])
 
-        loop(nz - 1, right_slots)
-        loop(nexp - 1, lambda k: right_copy(k + 1).start())
+        burst(nz - 1, right_slots)
+        burst(nexp - 1, lambda k: right_copy(k + 1).start())
         qrecv[j] = qsend[j]
         sent.append(lambda: loop(nexp - 1, lambda k: right_copy(k + 1).wait_send()))
 
@@ -657,7 +662,7 @@
         )
 
     group = hold // 2
-    loop(nexp - 1, left_arrive)
+    burst(nexp - 1, left_arrive)
     rows_v[0:hold, rows_part(z), :] = arranged(lrecv[...])
     for g in range(2):
         for n in range(1, nz):
@@ -671,7 +676,7 @@
             e = e_next(k + 1)
             remote(qsend.at[e], qrecv.at[e], qs_sem.at[0, 0], qr_sem.at[0, e], partner).wait_recv()
 
-        loop(nexp - 1, one)
+        burst(nexp - 1, one)
 
     def right_rows(k):
         rows_v[hold:parts, rows_part(z_next(k)), :] = arranged(qrecv[:, k])
@@ -706,10 +711,11 @@
         columns = tile_columns(n)
         acc_v[:, columns] = product(0, group, columns)
 
-    loop(tiles, lift_first)
+    for n in range(tiles):
+        lift_first(n)
     group_arrive(1)
     right_arrive()
-    loop(nz, right_rows)
+    burst(nz, right_rows)
     for g in range(2):
         right_forward(g).start()
 
@@ -728,7 +734,8 @@
         columns = tile_columns(n)
         acc_v[:, columns] += product(group, group, columns)
 
-    loop(tiles, lift_second)
+    for n in range(tiles):
+        lift_second(n)
     for g in range(2):
         right_forward(g).wait_recv()
 
@@ -737,7 +744,8 @@
         lifted = acc_v[:, columns] + product(hold, hold, columns)
         lifted_v[:, columns] = (lifted / (1.0 + jnp.exp(-lifted))).astype(BF16)
 
-    loop(tiles, lift_right)
+    for n in range(tiles):
+        lift_right(n)
     loop(chunks, lambda k: down_copy(k).wait())
 
     halves = chunks // 2
@@ -778,11 +786,12 @@
         rrecv[k, z] = rsend[k, z]
 
     ahead = halves // 2
-    loop(ahead, lambda n: lower(halves + n))
+    for n in range(ahead):
+        lower(halves + n)
     for n in range(halves):
         lower(n)
-    loop(ahead, send_back)
-    loop(halves - 1, keep_right)
+    burst(ahead, send_back)
+    burst(halves - 1, keep_right)
     lower(halves + ahead)
     keep_right(halves - 1)
 
@@ -808,10 +817,10 @@
     def home_right(k):
         qsend2[:, k] = unarranged(rsum[:, z_next(k)])
 
-    loop(nz - 1, lambda k: home_right(k + 1))
-    loop(nexp - 1, lambda k: home_right_copy(k + 1, True).start())
+    burst(nz - 1, lambda k: home_right(k + 1))
+    burst(nexp - 1, lambda k: home_right_copy(k + 1, True).start())
     home_right(0)
-    loop(nexp - 1, lambda k: home_right_copy(k + 1, False).start())
+    burst(nexp - 1, lambda k: home_right_copy(k + 1, False).start())
     qrecv2[j] = qsend2[j]
     sent.append(
         lambda: loop(
@@ -820,8 +829,9 @@
         )
     )
 
-    loop(halves - ahead - 1, lambda n: lower(n + halves + ahead + 1))
-    loop(halves - ahead, lambda n: send_back(n + ahead))
+    for n in range(halves + ahead + 1, 2 * halves):
+        lower(n)
+    burst(halves - ahead, lambda n: send_back(n + ahead))
 
     def drain_back(k):
         for n in range(1, nz):
@@ -842,14 +852,14 @@
         for q in range(2):
             lsum[2 * k + q] = total[:, q * wide : (q + 1) * wide].astype(BF16)
 
-    loop(halves, back_arrive)
+    burst(halves, back_arrive)
     lsend2[...] = unarranged(lsum[...])
 
     def home_left_copy(k):
         e = e_next(k)
         return remote(lsend2.at[e], lrecv2.at[j], hl_sem.at[0, k], hl_sem.at[1, j], at_e(e))
 
-    loop(nexp - 1, lambda k: home_left_copy(k + 1).start())
+    burst(nexp - 1, lambda k: home_left_copy(k + 1).start())
     lrecv2[j] = lsend2[j]
     sent.append(lambda: loop(nexp - 1, lambda k: home_left_copy(k + 1).wait_send()))
 
@@ -866,7 +876,7 @@
                 partner,
             ).wait_recv()
 
-        loop(nexp - 1, one)
+        burst(nexp - 1, one)
 
     home_right_arrive(0)
 
@@ -897,7 +907,7 @@
             at = (0 if first else hold) + k
             out_ref[:, at * wide : (at + 1) * wide] = rows[k * mine : (k + 1) * mine].astype(BF16)
 
-    loop(nexp - 1, home_left_arrive)
+    burst(nexp - 1, home_left_arrive)
     give(True, stream_v[0:stacked] + weighed(z, lrecv2[...]))
     for k in range(1, nz):
         zz = z_next(k)

time: 72.5 us -> 71 us (0.979)
  Pallas kernels: 70.9 us -> 69.4 us
    pallas_call x1, Pallas kernels: 70.9 us -> 69.4 us  [shards(): pl.pallas_call(functools.partial(kernel, nctx, nexp), out_shape=jax.Shape...]
where the time goes in v3:
time: 71 us; the launch traced here: 70.9 us
  Pallas kernels  69.4 us (98%)
  local copies, waits for them, and re-layouts  1.47 us (2%)
    pallas_call x1, Pallas kernels, shards(): pl.pallas_call(functools.partial(kernel, nctx, nexp), out_shape=jax.Shape...  69.4 us
    unnamed x1, local copies, waits for them, and re-layouts  1.47 us

profile of v3, /device:TPU:0, one launch (start us, length us, event | category | flops | bytes accessed | tf_op | source)
XLA Modules:
  0.0 70.9 jit_solution(2688597904452156651)
XLA Ops:
  0.0 69.4 %shard_map.136 = bf16[8,4096]{1,0:T(8,128)(2,1)} custom-call(bf16[128,512]{1,0:T(8,128)(2,1)} %x_hbm.1, bf16[128,512]{1,0:T(8,128)(2,1)} %gate_hbm.1, bf16[128,512]{1,0:T(8,128)(2,1)} %step_hbm.1, f32[16,128]{1,0:T(8,128)} %bitcast.13, f32[16,128]{1,0:T(8,128)} %bitcast.14, f32[16,512]{1,0:T(8,128)} %bitcast.11, f32[1,512]{1,0:T(1,128)} %bitcast.15, ...), custom_call_target="tpu_custom_call" | custom-call | tf_op jit(solution)/shard_map/pallas_call | solution.py:1067
  69.4 1.5 %copy.16 = bf16[8,4096]{1,0:T(8,128)(2,1)} copy(bf16[8,4096]{1,0:T(8,128)(2,1)} %shard_map.136) | data formatting | bytes 131072

commit v4 on v3

--- a/solution.py
+++ b/solution.py
@@ -792,7 +792,8 @@
         lower(n)
     burst(ahead, send_back)
     burst(halves - 1, keep_right)
-    lower(halves + ahead)
+    for n in range(halves + ahead, 2 * halves):
+        lower(n)
     keep_right(halves - 1)
 
     def unarranged(rows):
@@ -829,8 +830,6 @@
         )
     )
 
-    for n in range(halves + ahead + 1, 2 * halves):
-        lower(n)
     burst(halves - ahead, lambda n: send_back(n + ahead))
 
     def drain_back(k):

time: 71 us -> 71 us (level)
  no operation moved by 1% of the time
where the time goes in v4:
time: 71 us; the launch traced here: 70.9 us
  Pallas kernels  69.4 us (98%)
  local copies, waits for them, and re-layouts  1.47 us (2%)
    pallas_call x1, Pallas kernels, shards(): pl.pallas_call(functools.partial(kernel, nctx, nexp), out_shape=jax.Shape...  69.4 us
    unnamed x1, local copies, waits for them, and re-layouts  1.47 us

profile of v4, /device:TPU:0, one launch (start us, length us, event | category | flops | bytes accessed | tf_op | source)
XLA Modules:
  0.0 70.9 jit_solution(14811081267217452354)
XLA Ops:
  0.0 69.4 %shard_map.136 = bf16[8,4096]{1,0:T(8,128)(2,1)} custom-call(bf16[128,512]{1,0:T(8,128)(2,1)} %x_hbm.1, bf16[128,512]{1,0:T(8,128)(2,1)} %gate_hbm.1, bf16[128,512]{1,0:T(8,128)(2,1)} %step_hbm.1, f32[16,128]{1,0:T(8,128)} %bitcast.13, f32[16,128]{1,0:T(8,128)} %bitcast.14, f32[16,512]{1,0:T(8,128)} %bitcast.11, f32[1,512]{1,0:T(1,128)} %bitcast.15, ...), custom_call_target="tpu_custom_call" | custom-call | tf_op jit(solution)/shard_map/pallas_call | solution.py:1066
  69.4 1.5 %copy.16 = bf16[8,4096]{1,0:T(8,128)(2,1)} copy(bf16[8,4096]{1,0:T(8,128)(2,1)} %shard_map.136) | data formatting | bytes 131072
